TPU v7x, 256 devices: a whole 4x4x8 slice. The times are simulated.
256 devices in a mesh: row: 64 (over y, z, core), col: 4 (over x).
Axes of the slice: x: 4, y: 4, z: 8, core: 2. Of those that a mesh axis runs over, the one named last changes fastest.
Arguments:
- entity_feats: bfloat16 [65536, 256], P(('col', 'row')), may hold values from -6 to 6
- class_map: int32 [65536], P(('col', 'row')), may hold values from 0 to 127, as said below
- tile_values: bfloat16 [8192, 128, 128], P(('row', 'col')), may hold values from -0.09375 to 0.09375
- tile_rows: int32 [8192], P(('row', 'col')), may hold values from 0 to 3
- tile_column_index: int32 [8192], P(('row', 'col')), may hold values from 0 to 63
- tile_rels: int32 [8192], P(('row', 'col')), may hold values from 0 to 499
- tile_counts: int32 [256], P(('row', 'col')), may hold values from 4 to 32, as said below
- coefficients: bfloat16 [500, 8], replicated, may hold values from -2 to 2
- bases: bfloat16 [8, 256, 256], replicated, may hold values from -0.375 to 0.375
- cotangent: bfloat16 [32768, 256], P(('row', 'col')), may hold values from -6 to 6
Outputs:
- layer_out: bfloat16 [32768, 256], P(('row', 'col'))
- grad_entities: float32 [65536, 256], P(('col', 'row'))
- grad_bases: float32 [8, 256, 256], replicated
- grad_coef: float32 [500, 8], replicated
Inputs may be any that keep to these rules, and one draw needn't show every extreme that they name: `class_map`: within every block of 256 entities, every class number 0 to 127 occurs at least once. `tile_counts`: tile slots of a device from its count onward are unused; some device has all 32 slots live in every draw.
All inputs are finite; a program needn't handle non-finite values.
Results may differ from a plain program's by a relative error of at most 0.006.
Values may be sent and summed in bfloat16 or wider, within the bound.
No kernel may reach another device: no remote copies, remote signals or barrier semaphores. Data moves between devices by JAX's collectives and lax.ppermute only.
A program may use at most 128 MiB of HBM per device.

v0:
```python
import jax
import jax.numpy as jnp
from jax import lax
from jax.sharding import PartitionSpec as P

TBLK = 32


def tile_weights(rel_block, row_block, live, coefficients, trows, relations):
    pick_rel = (rel_block[:, None] == jnp.arange(relations, dtype=jnp.int32)[None, :]).astype(
        jnp.bfloat16
    )
    coef_rows = jnp.dot(pick_rel, coefficients, preferred_element_type=jnp.float32)
    pick_row = (
        (row_block[:, None] == jnp.arange(trows, dtype=jnp.int32)[None, :]) & live[:, None]
    ).astype(jnp.float32)
    weights = (pick_row[:, :, None] * coef_rows[:, None, :]).astype(jnp.bfloat16)
    return (weights, pick_row)


def local(
    entity_feats,
    class_map,
    tile_values,
    tile_rows,
    tile_column_index,
    tile_rels,
    tile_counts,
    coefficients,
    bases,
    cotangent,
):
    n_row = lax.axis_size("row")
    n_col = lax.axis_size("col")
    node_dev = cotangent.shape[0]
    tile = tile_values.shape[1]
    nbases = bases.shape[0]
    width = bases.shape[1]
    relations = coefficients.shape[0]
    rblock = node_dev * n_col
    cblock = node_dev * n_row
    trows = rblock // tile
    tile_column_list = cblock // tile
    member = class_map[:, None] == jnp.arange(node_dev, dtype=jnp.int32)[None, :]
    member_bf = member.astype(jnp.bfloat16)
    sums = lax.dot_general(
        member_bf, entity_feats, (((0,), (0,)), ((), ())), preferred_element_type=jnp.float32
    )
    counts = jnp.sum(member.astype(jnp.float32), axis=0)
    class_feat = (sums / counts[:, None]).astype(jnp.bfloat16)
    sender_device = lax.all_gather(class_feat, "row", axis=0, tiled=True).reshape(
        tile_column_list, tile, width
    )
    stacked = bases.reshape(nbases * width, width)
    live_count = tile_counts[0]
    turns = (live_count + TBLK - 1) // TBLK

    def forward_turn(step, carry):
        sums_acc, msg_store = carry
        leading_entry = step * TBLK
        live = leading_entry + jnp.arange(TBLK, dtype=jnp.int32) < live_count
        selected_entries = jnp.take(sender_device, tile_column_index, axis=0)
        messages = jnp.einsum(
            "kij,kjh->kih", tile_values, selected_entries, preferred_element_type=jnp.float32
        ).astype(jnp.bfloat16)
        weights, pick_row = tile_weights(tile_rels, tile_rows, live, coefficients, trows, relations)
        sums_acc = sums_acc + jnp.einsum(
            "ktb,kih->tibh", weights, messages, preferred_element_type=jnp.float32
        )
        msg_store = messages
        return (sums_acc, msg_store)

    init_sums = jnp.zeros((trows, tile, nbases, width), jnp.float32)
    init_store = jnp.zeros((tile_values.shape[0], tile, width), jnp.bfloat16)
    sums_acc, msg_store = lax.fori_loop(0, turns, forward_turn, (init_sums, init_store))
    part = sums_acc.astype(jnp.bfloat16).reshape(rblock, nbases * width)
    out_part = jnp.dot(part, stacked, preferred_element_type=jnp.float32)
    layer_out = lax.psum_scatter(out_part, "col", scatter_dimension=0, tiled=True).astype(
        jnp.bfloat16
    )
    dout_rows = lax.all_gather(cotangent, "col", axis=0, tiled=True)
    grads_rows = lax.dot_general(
        dout_rows, stacked, (((1,), (1,)), ((), ())), preferred_element_type=jnp.float32
    ).astype(jnp.bfloat16)
    dv_part = lax.dot_general(
        part, dout_rows, (((0,), (0,)), ((), ())), preferred_element_type=jnp.float32
    )
    grads_tiles = grads_rows.reshape(trows, tile, nbases, width)

    def backward_turn(step, carry):
        dcoef_acc, dx_acc = carry
        leading_entry = step * TBLK
        live = leading_entry + jnp.arange(TBLK, dtype=jnp.int32) < live_count
        weights, pick_row = tile_weights(tile_rels, tile_rows, live, coefficients, trows, relations)
        gram = jnp.einsum(
            "kih,tibh->ktb", msg_store, grads_tiles, preferred_element_type=jnp.float32
        )
        per_tile = jnp.sum(gram * pick_row[:, :, None], axis=1)
        dcoef_acc = dcoef_acc + jax.ops.segment_sum(per_tile, tile_rels, num_segments=relations)
        mixed = jnp.einsum(
            "ktb,tibh->kih", weights, grads_tiles, preferred_element_type=jnp.float32
        ).astype(jnp.bfloat16)
        back = jnp.einsum("kij,kih->kjh", tile_values, mixed, preferred_element_type=jnp.float32)
        dx_acc = dx_acc.at[tile_column_index].add(back)
        return (dcoef_acc, dx_acc)

    init_coef = jnp.zeros((relations, nbases), jnp.float32)
    init_dx = jnp.zeros((tile_column_list, tile, width), jnp.float32)
    dcoef_acc, dx_acc = lax.fori_loop(0, turns, backward_turn, (init_coef, init_dx))
    dx_all = dx_acc.reshape(cblock, width)
    dx_own = lax.psum_scatter(dx_all, "row", scatter_dimension=0, tiled=True)
    dv_sum, dcoef_sum = lax.psum((dv_part, dcoef_acc), ("row", "col"))
    scale = (node_dev * n_row * n_col) ** (-0.5)
    grad_bases = (dv_sum * scale).reshape(nbases, width, width)
    grad_coef = dcoef_sum * scale
    quotient = dx_own / counts[:, None]
    grad_entities = jnp.dot(member.astype(jnp.float32), quotient, precision=lax.Precision.HIGHEST)
    return (layer_out, grad_entities, grad_bases, grad_coef)


def solution(mesh):
    placed = (
        P(("col", "row"), None),
        P(("col", "row")),
        P(("row", "col"), None, None),
        P(("row", "col")),
        P(("row", "col")),
        P(("row", "col")),
        P(("row", "col")),
        P(),
        P(),
        P(("row", "col"), None),
    )
    return jax.shard_map(
        local,
        mesh=mesh,
        in_specs=placed,
        out_specs=(P(("row", "col"), None), P(("col", "row"), None), P(), P()),
        check_vma=False,
    )
```

profile of v0, /device:TPU:2, one launch (start us, length us, event | category | flops | bytes accessed | tf_op | source)
XLA Modules:
  0.0 570.0 jit_solution(12668102719578885372)
XLA Ops:
  7.2 0.0 copy-start
  7.2 0.0 all-gather.2.cloned.1.call-start
  7.2 0.9 convert_reduce_fusion
  8.1 1.8 fusion.22
  9.9 0.0 all-gather.2.cloned.1.call-update
  10.0 0.0 all-reduce.2.cloned.1.call-start
  10.7 12.6 %all_gather.7 = bf16[512,256]{1,0:T(8,128)(2,1)S(1)} all-gather(bf16[128,256]{1,0:T(8,128)(2,1)} %param.23), channel_id=1, replica_groups=mesh['row'=64,'col'=4] {'col'}, dimensions={0}, use_global_device_ids=true | all-gather | bytes 327680 | tf_op jit(solution)/shard_map/all_gather | solution.py:81
  23.3 0.7 compare_select_fusion.1
  23.9 0.7 compare_and_fusion
  24.6 0.9 fusion.32
  25.5 67.9 %all-gather.2.cloned.1.call-done = bf16[8192,256]{1,0:T(8,128)(2,1)} async-done(((bf16[128,256]{1,0:T(8,128)(2,1)}), bf16[8192,256]{1,0:T(8,128)(2,1)}) %all-gather.2.cloned.1.call-update) | async-done | bytes 4194320 | tf_op jit(solution)/shard_map/all_gather | solution.py:51
  93.4 4.3 gather_fusion
  97.7 0.0 copy-done.3
  97.7 3.8 convert_bitcast_fusion
  101.4 3.4 copy.35
  104.8 1.6 broadcast_in_dim.33
  106.4 2.3 broadcast_in_dim.32
  108.7 0.0 copy-done.8
  108.7 6.6 %while.31 = (s32[]{:T(128)}, f32[4,128,8,256]{3,2,1,0:T(8,128)}, bf16[32,128,256]{2,0,1:T(8,128)(2,1)}, s32[]{:T(128)}, s32[32]{0:T(128)S(1)}, /*index=5*/s32[]{...) while((s32[]{:T(128)}, f32[4,128,8,256]{3,2,1,0:T(8,128)}, ...), condition=%wide.region_2.3_spmd, body=%wide.region_1.2_spmd.sunk | while | flops 68159936 | bytes 48236912 | solution.py:75
  108.7 0.7 add_compare_fusion.4
  109.4 0.0 copy-start.1
  109.4 1.3 copy.62
  110.7 1.6 copy-done.1
  112.3 1.1 bitcast_add_fusion.2
  113.4 1.9 copy-done.2
  115.3 2.4 convert_element_type.73
  117.7 0.7 copy.42
  118.4 1.3 copy-done.5
  119.8 2.1 fusion.37
  121.8 0.0 all-reduce.2.cloned.1.call-update
  121.9 0.0 reduce-scatter.3.cloned.1.call-start
  121.9 0.7 convolution_convert_fusion
  122.7 0.7 copy.43
  123.3 0.0 copy-start.7
  123.4 0.3 copy.36
  123.6 1.3 copy-done.7
  124.9 0.7 fusion.23
  125.6 0.9 copy-done.6
  126.5 1.5 fusion.36
  128.1 0.0 reduce-scatter.3.cloned.1.call-update
  128.1 0.0 reduce-scatter.5.cloned.1.call-start
  128.2 0.0 copy-start.9
  128.2 0.0 copy-start.11
  128.2 4.3 broadcast_in_dim.46
  132.4 22.2 %while.32 = (s32[]{:T(128)}, f32[500,8]{1,0:T(8,128)S(1)}, f32[64,128,256]{2,1,0:T(8,128)}, s32[]{:T(128)}, s32[32]{0:T(128)S(1)}, /*index=5*/s32[32]{0:T(128)S(...) while((s32[]{:T(128)}, f32[500,8]{1,0:T(8,128)S(1)}, ...), condition=%wide.region_8.9_spmd, body=%wide.region_4.8_spmd.sunk | while | flops 337646112 | bytes 36713844 | solution.py:109
  132.4 0.7 add_compare_fusion.5
  133.1 0.1 copy.50
  133.2 0.8 scatter_fusion
  134.1 0.0 copy-start.4
  134.1 0.7 bitcast_convert_fusion.2
  134.8 0.5 copy-done.4
  135.3 3.7 convolution_bitcast_fusion.2
  139.0 5.6 copy.51
  144.6 10.1 %scatter_fusion.1 = f32[64,128,256]{2,1,0:T(8,128)} fusion(f32[64,128,256]{2,1,0:T(8,128)} %get-tuple-element.645, s32[32]{0:T(128)S(1)} %fusion.66, f32[32,128,256]{2,1,0:T(8,128)} %copy.51), kind=kCustom, calls=%fused_computation.2.clone.1 | custom fusion | flops 1048576 | bytes 12583040 | tf_op jit(solution)/shard_map/while/body/scatter-add | solution.py:104
  154.7 0.0 reduce-scatter.5.cloned.1.call-update
  154.7 0.1 copy.37
  154.8 75.1 %psum.15 = f32[500,8]{0,1:T(8,128)S(1)} all-reduce(f32[500,8]{0,1:T(8,128)S(1)} %copy.37), channel_id=1, replica_groups=mesh['row'=64,'col'=4] {'row','col'}, use_global_device_ids=true, to_apply=%region_11.12 | all-reduce | flops 4000 | bytes 32000 | tf_op jit(solution)/shard_map/psum | solution.py:112
  229.9 0.6 broadcast_multiply_fusion.1
  230.5 150.1 %all-reduce.2.cloned.1.call-done = f32[2048,256]{1,0:T(8,128)} async-done(((f32[2048,256]{1,0:T(8,128)}), f32[2048,256]{1,0:T(8,128)}) %all-reduce.2.cloned.1.call-update) | async-done | bytes 2097168 | tf_op jit(solution)/shard_map/psum | solution.py:112
  380.6 3.1 broadcast_multiply_fusion
  383.7 20.1 %reduce-scatter.3.cloned.1.call-done = f32[128,256]{1,0:T(8,128)} async-done(((f32[512,256]{1,0:T(8,128)}), f32[128,256]{1,0:T(8,128)}) %reduce-scatter.3.cloned.1.call-update) | async-done | bytes 131088 | tf_op jit(solution)/shard_map/reduce_scatter | solution.py:78
  403.8 1.5 convert_element_type.74
  405.3 156.1 %reduce-scatter.5.cloned.1.call-done = f32[128,256]{1,0:T(8,128)} async-done(((f32[8192,256]{1,0:T(8,128)}), f32[128,256]{1,0:T(8,128)}) %reduce-scatter.5.cloned.1.call-update) | async-done | bytes 131088 | tf_op jit(solution)/shard_map/reduce_scatter | solution.py:111
  561.5 2.0 fusion.27
  (16 shorter events, 0.1 us)
Async XLA Ops:
  7.2 114.7 %copy-start = (bf16[8,256,256]{2,1,0:T(8,128)(2,1)S(1)}, bf16[8,256,256]{2,1,0:T(8,128)(2,1)}, u32[]{:S(2)}) copy-start(bf16[8,256,256]{2,1,0:T(8,128)(2,1)} %param.22) | copy-start | bytes 3145732
  7.2 86.2 %all-gather.2.cloned.1.call-start = ((), (), s32[]{:S(2)}) async-start(), calls=%async_computation.2 | async-start | bytes 4259840 | tf_op jit(solution)/shard_map/all_gather | solution.py:51
  10.0 370.7 %all-reduce.2.cloned.1.call-start = ((), (), s32[]{:S(2)}) async-start(), calls=%async_computation.5 | async-start | bytes 4194304 | tf_op jit(solution)/shard_map/psum | solution.py:112
  93.4 4.3 copy-start.3
  106.4 2.3 copy-start.8
  109.4 2.9 copy-start.1
  113.4 1.9 copy-start.2
  118.4 1.3 copy-start.5
  121.9 282.0 %reduce-scatter.3.cloned.1.call-start = ((), (), s32[]{:S(2)}) async-start(), calls=%async_computation.3 | async-start | bytes 655360 | tf_op jit(solution)/shard_map/reduce_scatter | solution.py:78
  123.3 1.6 copy-start.7
  124.9 1.6 copy-start.6
  128.1 433.4 %reduce-scatter.5.cloned.1.call-start = ((), (), s32[]{:S(2)}) async-start(), calls=%async_computation.4 | async-start | bytes 8519680 | tf_op jit(solution)/shard_map/reduce_scatter | solution.py:111
  128.2 4.3 copy-start.9
  128.2 4.3 copy-start.11
  134.1 1.2 copy-start.4
  230.5 331.0 %copy-start.10 = (s32[256]{0:T(256)S(1)}, s32[256]{0:T(256)}, u32[]{:S(2)}) copy-start(s32[256]{0:T(256)} %param.15) | copy-start | bytes 3076
Sparse Core Ops, SparseCore 0:
  11.4 81.9 all-gather.1
  122.0 258.6 all-reduce.1
  383.2 20.6 reduce-scatter.2
  407.9 153.5 reduce-scatter.4
where the time goes:
time: 571 us; the launch traced here: 570 us
  waiting for transfers between devices  394 us (69%)
  blocking collectives  87.6 us (15%)
  local copies, waits for them, and re-layouts  32.2 us (6%)
  other arithmetic  22.1 us (4%)
  matrix products  18.9 us (3%)
  between operations  14.5 us (3%)
    reduce_scatter x1, waiting for transfers between devices, local(): dx_own = lax.psum_scatter(dx_all, 'row', scatter_dimension=0, tiled=True)  156 us
    psum x1, waiting for transfers between devices, local(): dv_sum, dcoef_sum = lax.psum((dv_part, dcoef_acc), ('row', 'col'))  150 us
    psum x1, blocking collectives, local(): dv_sum, dcoef_sum = lax.psum((dv_part, dcoef_acc), ('row', 'col'))  75.1 us
    all_gather x1, waiting for transfers between devices, local(): lax.all_gather(class_feat, 'row', axis=0, tiled=True)  67.9 us
    reduce_scatter x1, waiting for transfers between devices, local(): lax.psum_scatter(out_part, 'col', scatter_dimension=0, tiled=True)  20.1 us
    all_gather x1, blocking collectives, local(): dout_rows = lax.all_gather(cotangent, 'col', axis=0, tiled=True)  12.6 us
  transfers between devices with their start and end apart: 4, of which 4 were waited for; matrix products, arithmetic and copies ran while one was open for 7% of the time, Pallas kernels for 0%

commit v1 on v0

--- a/solution.py
+++ b/solution.py
@@ -4,6 +4,27 @@
 from jax.sharding import PartitionSpec as P
 
 TBLK = 32
+
+
+def in_order(pieces, dim):
+    pieces = jnp.moveaxis(pieces, 0, dim)
+    shape = pieces.shape
+    return pieces.reshape(*shape[:dim], shape[dim] * shape[dim + 1], *shape[dim + 2 :])
+
+
+def doubled(value, axis):
+    length, index = (lax.axis_size(axis), lax.axis_index(axis))
+    blocks, bit = (value[None], 1)
+    while bit < length:
+        other = lax.ppermute(blocks, axis, [(i, i ^ bit) for i in range(length)])
+        low = index & bit == 0
+        blocks = jnp.concatenate([jnp.where(low, blocks, other), jnp.where(low, other, blocks)])
+        bit *= 2
+    return blocks
+
+
+def gather_by_bits(x, axis, dim):
+    return in_order(doubled(x, axis), dim)
 
 
 def tile_weights(rel_block, row_block, live, coefficients, trows, relations):
@@ -48,9 +69,7 @@
     )
     counts = jnp.sum(member.astype(jnp.float32), axis=0)
     class_feat = (sums / counts[:, None]).astype(jnp.bfloat16)
-    sender_device = lax.all_gather(class_feat, "row", axis=0, tiled=True).reshape(
-        tile_column_list, tile, width
-    )
+    sender_device = gather_by_bits(class_feat, "row", 0).reshape(tile_column_list, tile, width)
     stacked = bases.reshape(nbases * width, width)
     live_count = tile_counts[0]
     turns = (live_count + TBLK - 1) // TBLK

time: 571 us -> 451 us (0.79)
  waiting for transfers between devices: 394 us -> 247 us
  starting transfers between devices: 0.16 us -> 16.8 us
  other arithmetic: 22.1 us -> 28.5 us
    reduce_scatter x1, waiting for transfers between devices: 156 us -> 0.01 us  [local(): dx_own = lax.psum_scatter(dx_all, 'row', scatter_dimension=0, tiled=True)]
    ppermute x0 -> x6, waiting for transfers between devices: none -> 92.9 us  [doubled(): other = lax.ppermute(blocks, axis, [(i, i ^ bit) for i in range(length)])]
    all_gather x1 -> x0, waiting for transfers between devices: 67.9 us -> none  [local(): lax.all_gather(class_feat, 'row', axis=0, tiled=True)]
    reduce_scatter x1, waiting for transfers between devices: 20.1 us -> 0.01 us  [local(): lax.psum_scatter(out_part, 'col', scatter_dimension=0, tiled=True)]
    ppermute x0 -> x6, starting transfers between devices: none -> 16.5 us  [doubled(): other = lax.ppermute(blocks, axis, [(i, i ^ bit) for i in range(length)])]
  transfers between devices with their start and end apart: 4 -> 9, of which waited for: 4 -> 7; matrix products, arithmetic and copies ran while one was open for 7% -> 8% of each run, Pallas kernels for 0% -> 0%
where the time goes in v1:
time: 451 us; the launch traced here: 450 us
  waiting for transfers between devices  247 us (55%)
  blocking collectives  90.6 us (20%)
  local copies, waits for them, and re-layouts  32.7 us (7%)
  other arithmetic  28.5 us (6%)
  matrix products  17.6 us (4%)
  starting transfers between devices  16.8 us (4%)
  between operations  16.4 us (4%)
    psum x1, waiting for transfers between devices, local(): dv_sum, dcoef_sum = lax.psum((dv_part, dcoef_acc), ('row', 'col'))  154 us
    ppermute x6, waiting for transfers between devices, doubled(): other = lax.ppermute(blocks, axis, [(i, i ^ bit) for i in range(length)])  92.9 us
    psum x1, blocking collectives, local(): dv_sum, dcoef_sum = lax.psum((dv_part, dcoef_acc), ('row', 'col'))  78.3 us
    ppermute x6, starting transfers between devices, doubled(): other = lax.ppermute(blocks, axis, [(i, i ^ bit) for i in range(length)])  16.5 us
    all_gather x1, blocking collectives, local(): dout_rows = lax.all_gather(cotangent, 'col', axis=0, tiled=True)  12.3 us
    scatter-add x1, other arithmetic, backward_turn(): dx_acc = dx_acc.at[tile_column_index].add(back)  10.1 us
  transfers between devices with their start and end apart: 9, of which 7 were waited for; matrix products, arithmetic and copies ran while one was open for 8% of the time, Pallas kernels for 0%

profile of v1, /device:TPU:2, one launch (start us, length us, event | category | flops | bytes accessed | tf_op | source)
XLA Modules:
  0.0 450.0 jit_solution(7589730505519121256)
XLA Ops:
  8.1 0.9 convert_reduce_fusion
  8.9 1.2 fusion.23
  10.1 0.1 collective-permute-start
  10.3 1.2 collective-permute-done
  11.5 2.0 collective-permute-start.1
  13.5 3.8 collective-permute-done.1
  17.4 3.4 collective-permute-start.2
  20.8 11.6 %collective-permute-done.2 = bf16[4,128,256]{2,1,0:T(8,128)(2,1)S(1)} collective-permute-done((bf16[4,128,256]{2,1,0:T(8,128)(2,1)S(1)}, bf16[4,128,256]{2,1,0:T(8,128)(2,1)S(1)}, u32[]{:S(2)}, u32[]{:S(2)}) %collective-permute-start.2) | collective-permute-done | bytes 262176 | tf_op jit(solution)/shard_map/ppermute | solution.py:19
  32.5 6.3 %collective-permute-start.3 = (bf16[8,128,256]{2,1,0:T(8,128)(2,1)S(1)}, bf16[8,128,256]{2,1,0:T(8,128)(2,1)S(1)}, u32[]{:S(2)}, u32[]{:S(2)}) collective-permute-start(bf16[8,128,256]{2,1,0:T(8,128)(2,1)S(1)} %pad_maximum_fusion.3), channel_id=1, source_target_pairs={{0,32},{4,36},{8,40},{12,44},{16,48},{20,52},{24,56},{28,60},{32,0... | collective-permute-start | bytes 1572872 | tf_op jit(solution)/shard_map/ppermute | solution.py:19
  38.8 23.0 %collective-permute-done.3 = bf16[8,128,256]{2,1,0:T(8,128)(2,1)S(1)} collective-permute-done((bf16[8,128,256]{2,1,0:T(8,128)(2,1)S(1)}, bf16[8,128,256]{2,1,0:T(8,128)(2,1)S(1)}, u32[]{:S(2)}, u32[]{:S(2)}) %collective-permute-start.3) | collective-permute-done | bytes 524320 | tf_op jit(solution)/shard_map/ppermute | solution.py:19
  61.7 0.1 broadcast_select_fusion.5
  61.8 0.8 copy-done.9
  62.6 0.1 pad_maximum_fusion.2
  62.7 0.0 copy-done.10
  62.8 1.6 collective-permute-start.4
  64.4 22.4 %collective-permute-done.4 = bf16[16,128,256]{2,1,0:T(8,128)(2,1)} collective-permute-done((bf16[16,128,256]{2,1,0:T(8,128)(2,1)S(1)}, bf16[16,128,256]{2,1,0:T(8,128)(2,1)}, u32[]{:S(2)}, u32[]{:S(2)}) %collective-permute-start.4) | collective-permute-done | bytes 1048608 | tf_op jit(solution)/shard_map/ppermute | solution.py:19
  86.8 1.7 broadcast_select_fusion.3
  88.5 1.5 pad_maximum_fusion.1
  90.0 3.2 collective-permute-start.5
  93.9 12.3 %all_gather.3 = bf16[512,256]{1,0:T(8,128)(2,1)S(1)} all-gather(bf16[128,256]{1,0:T(8,128)(2,1)S(1)} %copy-done.11), channel_id=1, replica_groups=mesh['row'=64,'col'=4] {'col'}, dimensions={0}, use_global_device_ids=true | all-gather | bytes 327680 | tf_op jit(solution)/shard_map/all_gather | solution.py:100
  106.3 0.2 fusion.33
  106.5 30.8 %collective-permute-done.5 = bf16[32,128,256]{2,1,0:T(8,128)(2,1)} collective-permute-done((bf16[32,128,256]{2,1,0:T(8,128)(2,1)}, bf16[32,128,256]{2,1,0:T(8,128)(2,1)}, u32[]{:S(2)}, u32[]{:S(2)}) %collective-permute-start.5) | collective-permute-done | bytes 2097184 | tf_op jit(solution)/shard_map/ppermute | solution.py:19
  137.3 1.9 broadcast_select_fusion.1
  139.2 2.3 pad_maximum_fusion
  141.5 4.3 gather_fusion
  145.8 3.8 convert_bitcast_fusion
  149.5 3.4 copy.36
  153.0 1.6 broadcast_in_dim.35
  154.5 2.3 broadcast_in_dim.34
  156.9 6.7 %while.31 = (s32[]{:T(128)}, f32[4,128,8,256]{3,2,1,0:T(8,128)}, bf16[32,128,256]{2,0,1:T(8,128)(2,1)}, s32[]{:T(128)}, s32[32]{0:T(128)S(1)}, /*index=5*/s32[]{...) while((s32[]{:T(128)}, f32[4,128,8,256]{3,2,1,0:T(8,128)}, ...), condition=%wide.region_2.3_spmd, body=%wide.region_1.2_spmd.sunk | while | flops 68159936 | bytes 48236912 | solution.py:94
  156.9 0.7 add_compare_fusion.4
  157.5 1.3 copy.63
  158.9 1.6 copy-done.2
  160.5 1.1 bitcast_add_fusion.2
  161.6 2.0 copy-done.3
  163.5 2.4 convert_element_type.73
  165.9 0.7 copy.43
  166.6 1.3 copy-done.6
  167.9 2.1 fusion.38
  170.0 0.2 reduce-scatter.3.cloned.1.call-start
  170.3 0.7 convolution_convert_fusion
  171.0 0.7 copy.44
  171.7 0.3 copy.37
  172.0 1.3 copy-done.8
  173.3 0.7 fusion.24
  174.0 0.9 copy-done.7
  174.9 1.5 fusion.37
  176.5 0.0 reduce-scatter.5.cloned.1.call-start
  176.6 4.3 broadcast_in_dim.57
  180.8 21.8 %while.32 = (s32[]{:T(128)}, f32[500,8]{1,0:T(8,128)S(1)}, f32[64,128,256]{2,1,0:T(8,128)}, s32[]{:T(128)}, s32[32]{0:T(128)S(1)}, /*index=5*/s32[32]{0:T(128)S(...) while((s32[]{:T(128)}, f32[500,8]{1,0:T(8,128)S(1)}, ...), condition=%wide.region_8.9_spmd, body=%wide.region_4.8_spmd.sunk | while | flops 337646112 | bytes 32519512 | solution.py:128
  180.8 0.7 add_compare_fusion.5
  181.5 0.1 copy.51
  181.6 0.8 scatter_fusion
  182.5 0.7 bitcast_convert_fusion.2
  183.2 3.7 convolution_bitcast_fusion.2
  186.9 5.7 %copy.52 = f32[32,128,256]{2,1,0:T(8,128)} copy(f32[32,128,256]{1,2,0:T(8,128)} %convolution_bitcast_fusion.2) | data formatting | bytes 8388608 | tf_op jit(solution)/shard_map/while/body/kij,kih->kjh/dot_general | solution.py:122
  192.5 10.1 %scatter_fusion.1 = f32[64,128,256]{2,1,0:T(8,128)} fusion(f32[64,128,256]{2,1,0:T(8,128)} %get-tuple-element.657, s32[32]{0:T(128)S(1)} %fusion.67, f32[32,128,256]{2,1,0:T(8,128)} %copy.52), kind=kCustom, calls=%fused_computation.2.clone.1 | custom fusion | flops 1048576 | bytes 12583040 | tf_op jit(solution)/shard_map/while/body/scatter-add | solution.py:123
  202.7 0.1 copy.38
  202.8 78.3 %psum.15 = f32[500,8]{0,1:T(8,128)S(1)} all-reduce(f32[500,8]{0,1:T(8,128)S(1)} %copy.38), channel_id=1, replica_groups=mesh['row'=64,'col'=4] {'row','col'}, use_global_device_ids=true, to_apply=%region_11.12 | all-reduce | flops 4000 | bytes 32000 | tf_op jit(solution)/shard_map/psum | solution.py:131
  281.1 0.6 broadcast_multiply_fusion.1
  281.7 154.3 %all-reduce.2.cloned.1.call-done = f32[2048,256]{1,0:T(8,128)} async-done(((f32[2048,256]{1,0:T(8,128)}), f32[2048,256]{1,0:T(8,128)}) %all-reduce.2.cloned.1.call-update) | async-done | bytes 2097168 | tf_op jit(solution)/shard_map/psum | solution.py:131
  436.0 3.1 broadcast_multiply_fusion
  439.1 1.5 convert_element_type.74
  440.6 2.0 fusion.28
  (47 shorter events, 0.4 us)
Async XLA Ops:
  8.0 162.3 %copy-start = (bf16[8,256,256]{2,1,0:T(8,128)(2,1)S(1)}, bf16[8,256,256]{2,1,0:T(8,128)(2,1)}, u32[]{:S(2)}) copy-start(bf16[8,256,256]{2,1,0:T(8,128)(2,1)} %param.22) | copy-start | bytes 3145732
  8.0 428.0 %all-reduce.2.cloned.1.call-start = ((), (), s32[]{:S(2)}) async-start(), calls=%async_computation.4 | async-start | bytes 4194304 | tf_op jit(solution)/shard_map/psum | solution.py:131
  10.1 1.3 collective-permute-start
  11.5 5.8 %collective-permute-start.1 = (bf16[2,128,256]{2,1,0:T(8,128)(2,1)S(1)}, bf16[2,128,256]{2,1,0:T(8,128)(2,1)S(1)}, u32[]{:S(2)}, u32[]{:S(2)}) collective-permute-start(bf16[2,128,256]{2,1,0:T(8,128)(2,1)S(1)} %pad_maximum_fusion.5), channel_id=1, source_target_pairs={{0,8},{4,12},{8,0},{12,4},{16,24},{20,28},{24,16},{28,20},{32,40},... | collective-permute-start | bytes 393224 | tf_op jit(solution)/shard_map/ppermute | solution.py:19
  17.4 15.0 %collective-permute-start.2 = (bf16[4,128,256]{2,1,0:T(8,128)(2,1)S(1)}, bf16[4,128,256]{2,1,0:T(8,128)(2,1)S(1)}, u32[]{:S(2)}, u32[]{:S(2)}) collective-permute-start(bf16[4,128,256]{2,1,0:T(8,128)(2,1)S(1)} %pad_maximum_fusion.4), channel_id=1, source_target_pairs={{0,16},{4,20},{8,24},{12,28},{16,0},{20,4},{24,8},{28,12},{32,48},... | collective-permute-start | bytes 786440 | tf_op jit(solution)/shard_map/ppermute | solution.py:19
  32.5 29.2 %collective-permute-start.3 = (bf16[8,128,256]{2,1,0:T(8,128)(2,1)S(1)}, bf16[8,128,256]{2,1,0:T(8,128)(2,1)S(1)}, u32[]{:S(2)}, u32[]{:S(2)}) collective-permute-start(bf16[8,128,256]{2,1,0:T(8,128)(2,1)S(1)} %pad_maximum_fusion.3), channel_id=1, source_target_pairs={{0,32},{4,36},{8,40},{12,44},{16,48},{20,52},{24,56},{28,60},{32,0... | collective-permute-start | bytes 1572872 | tf_op jit(solution)/shard_map/ppermute | solution.py:19
  61.8 0.8 copy-start.9
  61.8 1.0 copy-start.10
  62.8 24.1 %collective-permute-start.4 = (bf16[16,128,256]{2,1,0:T(8,128)(2,1)S(1)}, bf16[16,128,256]{2,1,0:T(8,128)(2,1)}, u32[]{:S(2)}, u32[]{:S(2)}) collective-permute-start(bf16[16,128,256]{2,1,0:T(8,128)(2,1)S(1)} %pad_maximum_fusion.2), channel_id=1, source_target_pairs={{0,64},{4,68},{8,72},{12,76},{16,80},{20,84},{24,88},{28,92},{32,9... | collective-permute-start | bytes 3145736 | tf_op jit(solution)/shard_map/ppermute | solution.py:19
  88.5 5.4 %copy-start.11 = (bf16[128,256]{1,0:T(8,128)(2,1)S(1)}, bf16[128,256]{1,0:T(8,128)(2,1)}, u32[]{:S(2)}) copy-start(bf16[128,256]{1,0:T(8,128)(2,1)} %param.23) | copy-start | bytes 196612
  88.5 17.7 %copy-start.16 = (s32[32]{0:T(128)S(1)}, s32[32]{0:T(128)}, u32[]{:S(2)}) copy-start(s32[32]{0:T(128)} %param.18) | copy-start | bytes 388
  88.5 17.8 %copy-start.13 = (s32[32]{0:T(128)S(1)}, s32[32]{0:T(128)}, u32[]{:S(2)}) copy-start(s32[32]{0:T(128)} %param.19) | copy-start | bytes 388
  88.5 17.8 %copy-start.14 = (bf16[500,8]{0,1:T(8,128)(2,1)S(1)}, bf16[500,8]{0,1:T(8,128)(2,1)}, u32[]{:S(2)}) copy-start(bf16[500,8]{0,1:T(8,128)(2,1)} %param.21) | copy-start | bytes 24004
  90.0 47.3 %collective-permute-start.5 = (bf16[32,128,256]{2,1,0:T(8,128)(2,1)}, bf16[32,128,256]{2,1,0:T(8,128)(2,1)}, u32[]{:S(2)}, u32[]{:S(2)}) collective-permute-start(bf16[32,128,256]{2,1,0:T(8,128)(2,1)} %pad_maximum_fusion.1), channel_id=1, source_target_pairs={{0,128},{4,132},{8,136},{12,140},{16,144},{20,148},{24,152},{28,15... | collective-permute-start | bytes 6291464 | tf_op jit(solution)/shard_map/ppermute | solution.py:19
  141.5 4.3 copy-start.4
  154.5 2.3 copy-start.12
  157.5 2.9 copy-start.2
  161.6 2.0 copy-start.3
  166.6 1.3 copy-start.6
  170.0 269.0 %reduce-scatter.3.cloned.1.call-start = ((), (), s32[]{:S(2)}) async-start(), calls=%async_computation.2 | async-start | bytes 655360 | tf_op jit(solution)/shard_map/reduce_scatter | solution.py:97
  171.7 1.6 copy-start.8
  173.3 1.6 copy-start.7
  176.5 264.1 %reduce-scatter.5.cloned.1.call-start = ((), (), s32[]{:S(2)}) async-start(), calls=%async_computation.3 | async-start | bytes 8519680 | tf_op jit(solution)/shard_map/reduce_scatter | solution.py:130
  176.5 4.3 copy-start.5
  281.1 161.5 %copy-start.1 = (bf16[8,256,256]{2,1,0:T(8,128)(2,1)S(1)}, bf16[8,256,256]{2,1,0:T(8,128)(2,1)}, u32[]{:S(2)}) copy-start(bf16[8,256,256]{2,1,0:T(8,128)(2,1)} %param.22) | copy-start | bytes 3145732
  281.7 158.9 %copy-start.15 = (s32[256]{0:T(256)S(1)}, s32[256]{0:T(256)}, u32[]{:S(2)}) copy-start(s32[256]{0:T(256)} %param.15) | copy-start | bytes 3076
Sparse Core Ops, SparseCore 0:
  170.2 265.7 all-reduce.1
Sparse Core Ops, SparseCore 1:
  176.6 22.9 reduce-scatter.2
  203.5 153.4 reduce-scatter.4
